TPU v7x, 32 devices: a whole 2x2x4 slice. The times are simulated.
32 devices in a mesh: groups: 2 (over y), tensor: 16 (over z, x, core).
Axes of the slice: x: 2, y: 2, z: 4, core: 2. Of those that a mesh axis runs over, the one named last changes fastest.
Arguments:
- layer_input: bfloat16 [256, 8192], P(('groups', 'tensor')), parts along dimension 0, may hold values from -6 to 6
- out_cotangent: bfloat16 [256, 8192], P(('groups', 'tensor')), parts along dimension 0, may hold values from -6 to 6
- gate_pre: bfloat16 [256, 28672], P('groups', 'tensor'), parts along dimension 0, may hold values from -8 to 8
- up_pre: bfloat16 [256, 28672], P('groups', 'tensor'), parts along dimension 0, may hold values from -6 to 6
- down_weight: bfloat16 [28672, 8192], P('tensor'), may hold values from -0.03125 to 0.03125
- proj_in_up: bfloat16 [8192, 64], replicated, may hold values from -0.0625 to 0.0625
- proj_out_up: bfloat16 [28672, 64], P('tensor'), may hold values from -0.03125 to 0.03125
- proj_in_down: bfloat16 [28672, 64], P('tensor'), may hold values from -0.03125 to 0.03125
- proj_out_down: bfloat16 [8192, 64], replicated, may hold values from -0.0625 to 0.0625
- owner_order: int32 [32], P('groups'), parts along dimension 0, may hold values from 0 to 15, each once
- query_features: bfloat16 [64, 8192], P(('groups', 'tensor')), parts along dimension 0, may hold values from -0.0625 to 0.0625
Outputs:
- logged: bfloat16 [32, 8192], P(('groups', 'tensor')), parts along dimension 0
- scores: float32 [32, 32], P(('groups', 'tensor')), parts along dimension 0
There are 2 independent parts, one for each index of `groups`. A program takes and returns all parts, laid end to end along the dimension named above; an argument that names none is the same for every part. Nothing has to cross between parts.
Inputs may be any that keep to these rules, and one draw needn't show every extreme that they name: `owner_order`: each example appears exactly once; logged row j is owned by device j // 1 of tensor.
All inputs are finite; a program needn't handle non-finite values.
Results may differ from a plain program's by a relative error of at most 0.0051.
Values may be sent and summed in bfloat16 or wider, within the bound.
A program may use at most 128 MiB of HBM per device.

v0:
```python
import jax
import jax.numpy as jnp
from jax import lax
from jax.sharding import PartitionSpec as P

LEN = 8


def outer_blocks(left, right):
    left = left.reshape(-1, LEN, left.shape[1])
    right = right.reshape(-1, LEN, right.shape[1])
    prod = jnp.einsum("elk,elm->ekm", left, right, precision=lax.Precision.HIGHEST)
    return prod.reshape(prod.shape[0], -1)


def shards(
    layer_input,
    out_cotangent,
    gate_pre,
    up_pre,
    down_weight,
    proj_in_up,
    proj_out_up,
    proj_in_down,
    proj_out_down,
    owner_order,
    query_features,
):
    own_in_up = jnp.dot(layer_input, proj_in_up, preferred_element_type=jnp.float32)
    own_out_down = jnp.dot(out_cotangent, proj_out_down, preferred_element_type=jnp.float32)
    in_up, out_down = (
        lax.all_gather(own_in_up, "tensor", axis=0, tiled=True),
        lax.all_gather(own_out_down, "tensor", axis=0, tiled=True),
    )
    joined = lax.dot_general(
        lax.all_gather(out_cotangent, "tensor", axis=0, tiled=True),
        down_weight,
        (((1,), (1,)), ((), ())),
        preferred_element_type=jnp.float32,
    )
    gate_act = jax.nn.silu(gate_pre.astype(jnp.float32))
    hidden = (gate_act * up_pre.astype(jnp.float32)).astype(jnp.bfloat16)
    grad_up = (joined * gate_act).astype(jnp.bfloat16)
    out_up = jnp.dot(grad_up, proj_out_up, preferred_element_type=jnp.float32)
    in_down = jnp.dot(hidden, proj_in_down, preferred_element_type=jnp.float32)
    partial_blocks = jnp.concatenate(
        [outer_blocks(out_up, in_up), outer_blocks(out_down, in_down)], axis=1
    )
    ordered = jnp.take(partial_blocks, owner_order, axis=0)
    summed = lax.psum_scatter(ordered, "tensor", scatter_dimension=0, tiled=True)
    logged = summed.astype(jnp.bfloat16)
    scores = lax.dot_general(
        logged,
        lax.all_gather(query_features, "tensor", axis=0, tiled=True),
        (((1,), (1,)), ((), ())),
        preferred_element_type=jnp.float32,
    )
    return (logged, scores)


def solution(mesh):
    placed = (
        P(("groups", "tensor"), None),
        P(("groups", "tensor"), None),
        P("groups", "tensor"),
        P("groups", "tensor"),
        P("tensor", None),
        P(),
        P("tensor", None),
        P("tensor", None),
        P(),
        P("groups"),
        P(("groups", "tensor"), None),
    )
    return jax.shard_map(
        shards,
        mesh=mesh,
        in_specs=placed,
        out_specs=(P(("groups", "tensor"), None), P(("groups", "tensor"), None)),
        check_vma=False,
    )
```

profile of v0, /device:TPU:0, one launch (start us, length us, event | category | flops | bytes accessed | tf_op | source)
XLA Modules:
  0.0 169.1 jit_solution(16714235157410169759)
XLA Ops:
  7.2 0.0 copy-start
  7.2 0.0 all-gather.3.cloned.1.call-start
  7.2 0.7 all-gather.3.cloned.1.call-update
  7.9 0.5 copy-done
  8.4 1.3 fusion.15
  9.7 23.4 %all_gather.14 = f32[128,64]{1,0:T(8,128)S(1)} all-gather(f32[8,64]{1,0:T(8,128)S(1)} %fusion.15), channel_id=1, replica_groups=mesh['groups'=2,'tensor'=16] {'tensor'}, dimensions={0}, use_global_device_ids=true | all-gather | bytes 34816 | tf_op jit(solution)/shard_map/all_gather | solution.py:33
  33.1 1.6 convolution_bitcast_fusion
  34.7 1.0 fusion.6
  35.7 0.2 reshape.36
  35.9 20.9 %all-gather = bf16[16,2,8192]{2,1,0:T(2,128)(2,1)S(1)} all-gather(bf16[1,2,8192]{2,1,0:T(2,128)(2,1)} %bitcast.27), channel_id=1, replica_groups=mesh['groups'=2,'tensor'=16] {'tensor'}, dimensions={0}, use_global_device_ids=true | all-gather | bytes 557056 | tf_op jit(solution)/shard_map/all_gather | solution.py:54
  56.8 0.2 reshape.48
  57.0 1.2 dynamic-slice
  58.3 1.7 fusion.14
  60.0 17.8 %all_gather.13 = f32[128,64]{1,0:T(8,128)S(1)} all-gather(f32[8,64]{1,0:T(8,128)S(1)} %fusion.14), channel_id=1, replica_groups=mesh['groups'=2,'tensor'=16] {'tensor'}, dimensions={0}, use_global_device_ids=true | all-gather | bytes 34816 | tf_op jit(solution)/shard_map/all_gather | solution.py:32
  77.8 0.7 compare_select_fusion
  78.4 0.7 compare_and_fusion
  79.1 15.3 %fusion.2 = f32[16,8,64]{2,1,0:T(8,128)S(1)} fusion(bf16[1792,64]{0,1:T(8,128)(2,1)} %param.17, bf16[128,8192]{1,0:T(8,128)(2,1)} %all-gather.3.cloned.1.call-done, bf16[1792,8192]{1,0:T(8,128)(2,1)} %param.15, bf16[128,1792]{1,0:T(8,128)(2,1)} %param.13), kind=kOutput, calls=%fused_computation.6 | convolution fusion | flops 3789062144 | bytes 32178176 | tf_op jit(solution)/shard_map/dot_general | solution.py:44
  94.4 1.0 fusion.8
  95.4 0.2 reshape.33
  95.6 0.7 gather_fusion
  96.4 0.1 broadcast_select_fusion
  96.5 64.4 %all-reduce.2 = bf16[16,8192]{1,0:T(8,128)(2,1)S(1)} all-reduce(f32[16,8192]{1,0:T(8,128)S(1)} %broadcast_select_fusion), channel_id=2, replica_groups=mesh['groups'=2,'tensor'=16] {'tensor'}, use_global_device_ids=true, to_apply=%region_0.1.clone | all-reduce | flops 131072 | bytes 786432
  160.8 0.7 dynamic-slice_convert_fusion
  161.5 0.8 fusion.10
  (5 shorter events, 0.1 us)
Async XLA Ops:
  7.2 1.2 copy-start
  7.2 71.9 %all-gather.3.cloned.1.call-start = ((), (), s32[]{:S(2)}) async-start(), calls=%async_computation | async-start | bytes 2228224 | tf_op jit(solution)/shard_map/all_gather | solution.py:36
  161.5 0.8 copy-start.1
Sparse Core Ops, SparseCore 0:
  10.2 45.6 all-gather.2
where the time goes:
time: 169 us
  blocking collectives  127 us (75%)
  matrix products  22.6 us (13%)
  between operations  14.1 us (8%)
  local copies, waits for them, and re-layouts  3.71 us (2%)
    unnamed x1, blocking collectives  64.4 us
    all_gather x1, blocking collectives, shards(): lax.all_gather(own_out_down, 'tensor', axis=0, tiled=True)  23.4 us
    all_gather x1, blocking collectives, shards(): lax.all_gather(query_features, 'tensor', axis=0, tiled=True)  20.9 us
    all_gather x1, blocking collectives, shards(): lax.all_gather(own_in_up, 'tensor', axis=0, tiled=True)  17.8 us
    dot_general x1, matrix products, shards(): out_up = jnp.dot(grad_up, proj_out_up, preferred_element_type=jnp.float32)  15.3 us
  transfers between devices with their start and end apart: 1, of which 0 were waited for; matrix products, arithmetic and copies ran while one was open for 5% of the time, Pallas kernels for 0%

commit v1 on v0

v1 whole, which is shorter than its diff:
```python
import functools

import jax
import jax.numpy as jnp
from jax import lax
from jax.experimental import pallas as pl
from jax.experimental.pallas import tpu as pltpu
from jax.sharding import PartitionSpec as P

LEN = 8
OUTER = 4
CHUNKS = 4
F32, BF16 = jnp.float32, jnp.bfloat16


def kernel(
    n,
    li_ref, oc_ref, gate_ref, up_ref, w_ref, piu_ref, pou_ref, pid_ref, pod_ref, order_ref, q_ref,
    logged_ref, scores_ref,
    li, oc, q, gate, up, w, piu, pou, pid, pod,
    g, x, acc, act, mine, all_u, in_down, part, stage, got, qtmp, rows,
    loc_sem, w_sem,
    z_send, z_recv, x_send, x_recv, c_send, c_recv, u_send, u_recv, r_send, r_recv,
):
    a_n, b_n = OUTER, n // (2 * OUTER)
    chunks = w.shape[0]
    width = w.shape[2]
    half = width // 2
    feat = w.shape[1]
    tile = 256 if feat % 256 == 0 else feat
    tiles = feat // tile
    side = pou.shape[1]
    me = lax.axis_index("tensor")
    core = lax.rem(me, 2)
    b = lax.rem(me // 2, b_n)
    a = me // (2 * b_n)
    slot = (core * b_n + b) * a_n + a

    def device(a_, b_, core_):
        return {"tensor": (a_ * b_n + b_) * 2 + core_}

    small = [(oc_ref, oc), (q_ref, q), (gate_ref, gate), (up_ref, up), (pid_ref, pid),
             (li_ref, li), (piu_ref, piu), (pod_ref, pod), (pou_ref, pou)]
    local = {}
    for i, (src, dst) in enumerate(small):
        local[i] = pltpu.make_async_copy(src, dst, loc_sem.at[i])
        local[i].start()
    w_copies = []
    for c in range(chunks):
        cp = pltpu.make_async_copy(w_ref.at[:, pl.ds(c * width, width)], w.at[c], w_sem.at[c])
        cp.start()
        w_copies.append(cp)

    barrier = pltpu.get_barrier_semaphore()

    @pl.loop(1, n)
    def _(k):
        pl.semaphore_signal(barrier, inc=1, device_id={"tensor": lax.rem(me + k, n)},
                            device_id_type=pl.DeviceIdType.MESH)

    local[0].wait()
    for c in range(chunks):
        lo = oc[:, c * width:c * width + half].astype(F32)
        hi = oc[:, c * width + half:(c + 1) * width].astype(F32)
        g[c, slot] = jnp.concatenate([lo, hi], axis=0).astype(BF16)
    local[1].wait()
    qn = q.shape[0]
    qs = 16 // qn
    qw = q.shape[1] // qs
    for s in range(qs):
        qtmp[s * qn:(s + 1) * qn, :] = q[:, s * qw:(s + 1) * qw].astype(F32)
    g[chunks, slot] = qtmp[...].astype(BF16)

    pl.semaphore_wait(barrier, n - 1)

    def z_copy(c, k):
        return pltpu.make_async_remote_copy(
            src_ref=g.at[c, slot], dst_ref=g.at[c, slot],
            send_sem=z_send.at[c, k], recv_sem=z_recv.at[c, k],
            device_id=device(lax.rem(a + k, a_n), b, core), device_id_type=pl.DeviceIdType.MESH)

    def x_copy(c, k):
        column = pl.ds((core * b_n + b) * a_n, a_n)
        return pltpu.make_async_remote_copy(
            src_ref=g.at[c, column], dst_ref=g.at[c, column],
            send_sem=x_send.at[c, k], recv_sem=x_recv.at[c, k],
            device_id=device(a, lax.rem(b + k, b_n), core), device_id_type=pl.DeviceIdType.MESH)

    def c_copy(c, k):
        column = pl.ds((core * b_n + lax.rem(b - k + b_n, b_n)) * a_n, a_n)
        return pltpu.make_async_remote_copy(
            src_ref=g.at[c, column], dst_ref=g.at[c, column],
            send_sem=c_send.at[c, k], recv_sem=c_recv.at[c, k],
            device_id=device(a, b, 1 - core), device_id_type=pl.DeviceIdType.MESH)

    for c in range(chunks + 1):
        for k in range(1, a_n):
            z_copy(c, k).start()

    def forward_z(c):
        for k in range(1, a_n):
            z_copy(c, k).wait_recv()
        for k in range(1, b_n):
            x_copy(c, k).start()
        c_copy(c, 0).start()

    def forward_x(c):
        for k in range(1, b_n):
            x_copy(c, k).wait_recv()
            c_copy(c, k).start()

    def arrived(c):
        for k in range(b_n):
            c_copy(c, k).wait_recv()

    for i in (2, 3, 4):
        local[i].wait()
    for i in range(tiles):
        sl = slice(i * tile, (i + 1) * tile)
        v = gate[:, sl].astype(F32)
        ga = v / (1.0 + jnp.exp(-v))
        act[:, sl] = ga
        hidden = (ga * up[:, sl].astype(F32)).astype(BF16)
        d = jnp.dot(hidden, pid[sl, :], preferred_element_type=F32)
        if i == 0:
            in_down[...] = d
        else:
            in_down[...] += d
    for i in (5, 6, 7):
        local[i].wait()
    own_iu = jnp.dot(li[...], piu[...], preferred_element_type=F32)
    own_od = jnp.dot(oc[...], pod[...], preferred_element_type=F32)
    own_u = jnp.concatenate([own_iu, own_od], axis=1)
    mine[...] = own_u
    all_u[me] = own_u

    def u_copy(k):
        return pltpu.make_async_remote_copy(
            src_ref=mine, dst_ref=all_u.at[me], send_sem=u_send.at[0], recv_sem=u_recv.at[0],
            device_id={"tensor": lax.rem(me + k, n)}, device_id_type=pl.DeviceIdType.MESH)

    @pl.loop(1, n)
    def _(k):
        u_copy(k).start()

    def pack(c):
        @pl.loop(0, n // 2)
        def _(i):
            s0 = lax.rem(i, b_n) * a_n + i // b_n
            g0 = g[c, s0].astype(F32)
            g1 = g[c, s0 + b_n * a_n].astype(F32)
            at = pl.ds(pl.multiple_of(i * 16, 16), 16)
            x[at, 0:half] = jnp.concatenate([g0[0:8], g1[0:8]], axis=0).astype(BF16)
            x[at, half:width] = jnp.concatenate([g0[8:16], g1[8:16]], axis=0).astype(BF16)

    nt = (((1,), (1,)), ((), ()))

    def multiply(c):
        w_copies[c].wait()
        arrived(c)
        pack(c)

        @pl.loop(0, tiles)
        def _(i):
            at = pl.ds(pl.multiple_of(i * tile, tile), tile)
            d = lax.dot_general(x[...], w[c, at, :], nt, preferred_element_type=F32)
            if c == 0:
                acc[i] = d
            else:
                acc[i] += d

    forward_z(0)
    for c in range(chunks):
        forward_z(c + 1)
        forward_x(c)
        multiply(c)

    local[8].wait()
    out_up = jnp.zeros((x.shape[0], side), F32)
    for i in range(tiles):
        sl = slice(i * tile, (i + 1) * tile)
        gu = (acc[i] * act[:, sl]).astype(BF16)
        out_up += jnp.dot(gu, pou[sl, :], preferred_element_type=F32)
    part[...] = jnp.concatenate([out_up, in_down[...]], axis=1).reshape(part.shape)

    def r_copy(k):
        to = lax.rem(me + k, n)
        return pltpu.make_async_remote_copy(
            src_ref=stage.at[to], dst_ref=got.at[me], send_sem=r_send.at[0], recv_sem=r_recv.at[0],
            device_id={"tensor": to}, device_id_type=pl.DeviceIdType.MESH)

    @pl.loop(1, n)
    def _(k):
        to = lax.rem(me + k, n)
        stage[to] = part[order_ref[to]]
        r_copy(k).start()

    got[me] = part[order_ref[me]]
    forward_x(chunks)

    def total(ref, send_sem, recv_sem):
        span = ref.at[pl.ds(0, n - 1)]
        return pltpu.make_async_remote_copy(
            src_ref=span, dst_ref=span, send_sem=send_sem.at[0], recv_sem=recv_sem.at[0],
            device_id={"tensor": lax.rem(me + 1, n)}, device_id_type=pl.DeviceIdType.MESH)

    total(all_u, u_send, u_recv).wait_recv()
    total(got, r_send, r_recv).wait_recv()
    summed = jnp.sum(got[...], axis=0)
    u = all_u[order_ref[me]]
    lane = lax.broadcasted_iota(jnp.int32, (LEN, 2 * side), 1)
    first = lane < side
    left = jnp.where(first, summed, u)
    right = jnp.where(first, u, summed)
    swapped = jnp.concatenate([right[:, side:], right[:, :side]], axis=1)
    right_up = jnp.where(first, right, swapped)
    right_down = jnp.where(first, swapped, right)
    per = qw // (2 * side)
    for p in range(side):
        rgt = right_up if p < side // 2 else right_down
        lft = jnp.where(first, left[:, 2 * p:2 * p + 1], left[:, 2 * p + 1:2 * p + 2])
        rows[p // per:p // per + 1, (p % per) * 2 * side:(p % per + 1) * 2 * side] = jnp.sum(
            lft * rgt, axis=0, keepdims=True)
    for s in range(qs):
        logged_ref[:, s * qw:(s + 1) * qw] = rows[s:s + 1, :].astype(BF16)

    arrived(chunks)
    gq = g[chunks].reshape(n * 16, qw)
    prod = lax.dot_general(rows[...].astype(BF16), gq, nt, preferred_element_type=F32)
    r_i = lax.broadcasted_iota(jnp.int32, (qs, n * 16), 1)
    s_i = lax.broadcasted_iota(jnp.int32, (qs, n * 16), 0)
    prod = jnp.where(lax.rem(r_i, 16) // qn == s_i, prod, 0.0)
    r_j = lax.broadcasted_iota(jnp.int32, (n * 16, n * qn), 0)
    c_j = lax.broadcasted_iota(jnp.int32, (n * 16, n * qn), 1)
    sl_j = r_j // 16
    dev_j = (lax.rem(sl_j, a_n) * b_n + lax.rem(sl_j // a_n, b_n)) * 2 + sl_j // (a_n * b_n)
    pick = jnp.where(dev_j * qn + lax.rem(r_j, qn) == c_j, 1.0, 0.0).astype(F32)
    sc = jnp.dot(prod, pick, preferred_element_type=F32, precision=lax.Precision.HIGHEST)
    scores_ref[...] = jnp.sum(sc, axis=0, keepdims=True)

    for c in range(chunks + 1):
        for k in range(1, a_n):
            z_copy(c, k).wait_send()
        for k in range(1, b_n):
            x_copy(c, k).wait_send()
        for k in range(b_n):
            c_copy(c, k).wait_send()
    total(all_u, u_send, u_recv).wait_send()
    total(got, r_send, r_recv).wait_send()


def shards(n, li, oc, gate, up, w, piu, pou, pid, pod, order, q):
    tokens, feat = gate.shape
    model = w.shape[1]
    side = piu.shape[1]
    width = model // CHUNKS
    tile = 256 if feat % 256 == 0 else feat
    b_n = n // (2 * OUTER)
    vm = pltpu.VMEM
    dma = pltpu.SemaphoreType.DMA
    anywhere = pl.BlockSpec(memory_space=pl.ANY)
    qn = q.shape[0]
    return pl.pallas_call(
        functools.partial(kernel, n),
        out_shape=(jax.ShapeDtypeStruct((1, q.shape[1]), BF16),
                   jax.ShapeDtypeStruct((1, n * qn), F32)),
        in_specs=[anywhere] * 9 + [pl.BlockSpec(memory_space=pltpu.SMEM), anywhere],
        out_specs=(pl.BlockSpec(memory_space=pltpu.VMEM),) * 2,
        scratch_shapes=[
            vm(li.shape, BF16), vm(oc.shape, BF16), vm(q.shape, BF16),
            vm(gate.shape, BF16), vm(up.shape, BF16), vm((CHUNKS, feat, width), BF16),
            vm(piu.shape, BF16), vm(pou.shape, BF16), vm(pid.shape, BF16), vm(pod.shape, BF16),
            vm((CHUNKS + 1, n, 16, width // 2), BF16),
            vm((tokens, width), BF16),
            vm((feat // tile, tokens, tile), F32),
            vm((tokens, feat), F32),
            vm((LEN, 2 * side), F32), vm((n, LEN, 2 * side), F32),
            vm((tokens, side), F32),
            vm((n, LEN, 2 * side), F32), vm((n, LEN, 2 * side), F32), vm((n, LEN, 2 * side), F32),
            vm((16, q.shape[1] * qn // 16), F32), vm((16 // qn, q.shape[1] * qn // 16), F32),
            dma((9,)), dma((CHUNKS,)),
            dma((CHUNKS + 1, OUTER)), dma((CHUNKS + 1, OUTER)),
            dma((CHUNKS + 1, b_n)), dma((CHUNKS + 1, b_n)),
            dma((CHUNKS + 1, b_n)), dma((CHUNKS + 1, b_n)),
            dma((1,)), dma((1,)), dma((1,)), dma((1,)),
        ],
        compiler_params=pltpu.CompilerParams(
            collective_id=0, has_side_effects=True, vmem_limit_bytes=60 * 1024 * 1024),
        cost_estimate=pl.CostEstimate(
            flops=2 * tokens * feat * model, bytes_accessed=2 * feat * model, transcendentals=tokens * feat),
    )(li, oc, gate, up, w, piu, pou, pid, pod, order, q)


def solution(mesh):
    rows = P(("groups", "tensor"), None)
    split = P("tensor", None)
    return jax.shard_map(
        functools.partial(shards, mesh.shape["tensor"]),
        mesh=mesh,
        in_specs=(rows, rows, P("groups", "tensor"), P("groups", "tensor"), split, P(), split, split, P(),
                  P("groups"), rows),
        out_specs=(rows, rows),
        check_vma=False,
    )
```

time: 169 us -> 54.3 us (0.32)
  blocking collectives: 127 us -> 0 us
  Pallas kernels: 0 us -> 43.2 us
  matrix products: 22.6 us -> 0 us
  between operations: 14.1 us -> 0.66 us
  local copies, waits for them, and re-layouts: 3.71 us -> 10.2 us
    unnamed x1 -> x0, blocking collectives: 64.4 us -> none
    all_gather x3 -> x0, blocking collectives: 62.2 us -> none  [the longest x1 23.4 us: shards(): lax.all_gather(own_out_down, 'tensor', axis=0, tiled=True)]
    pallas_call x0 -> x1, Pallas kernels: none -> 43.2 us  [shards(): pl.pallas_call(functools.partial(kernel, n), out_shape=(jax.ShapeDtypeStr...]
    dot_general x7 -> x0, matrix products: 22.6 us -> none  [the longest x1 15.3 us: shards(): out_up = jnp.dot(grad_up, proj_out_up, preferred_element_type=jnp.float32)]
    unnamed x6 -> x10, local copies, waits for them, and re-layouts: 1.93 us -> 10.2 us
  transfers between devices with their start and end apart: 1 -> 0, of which waited for: 0 -> 0; matrix products, arithmetic and copies ran while one was open for 5% -> 0% of each run, Pallas kernels for 0% -> 0%
where the time goes in v1:
time: 54.3 us; the launch traced here: 54 us
  Pallas kernels  43.2 us (80%)
  local copies, waits for them, and re-layouts  10.2 us (19%)
  between operations  0.66 us (1%)
    pallas_call x1, Pallas kernels, shards(): pl.pallas_call(functools.partial(kernel, n), out_shape=(jax.ShapeDtypeStr...  43.2 us
    unnamed x10, local copies, waits for them, and re-layouts  10.2 us

profile of v1, /device:TPU:0, one launch (start us, length us, event | category | flops | bytes accessed | tf_op | source)
XLA Modules:
  0.0 54.0 jit_solution(12234011635079693860)
XLA Ops:
  0.6 0.0 copy-start
  0.6 0.0 copy-start.1
  0.7 2.1 %copy.14.pou_ref = bf16[1792,64]{1,0:T(8,128)(2,1)} copy(bf16[1792,64]{0,1:T(8,128)(2,1)} %param.17) | data formatting | bytes 458752 | tf_op args[6]
  2.7 1.9 %copy.15.pid_ref = bf16[1792,64]{1,0:T(8,128)(2,1)} copy(bf16[1792,64]{0,1:T(8,128)(2,1)} %param.18) | data formatting | bytes 458752 | tf_op args[7]
  4.6 0.0 copy-done
  4.6 1.8 %copy.13.piu_ref = bf16[8192,64]{1,0:T(8,128)(2,1)} copy(bf16[8192,64]{0,1:T(8,128)(2,1)S(1)} %copy-done) | data formatting | bytes 2097152 | tf_op args[5]
  6.5 0.0 copy-done.1
  6.5 1.8 %copy.16.pod_ref = bf16[8192,64]{1,0:T(8,128)(2,1)} copy(bf16[8192,64]{0,1:T(8,128)(2,1)S(1)} %copy-done.1) | data formatting | bytes 2097152 | tf_op args[8]
  8.2 43.2 %shard_map.122 = (bf16[1,8192]{1,0:T(2,128)(2,1)}, f32[1,32]{1,0:T(1,128)}) custom-call(bf16[8,8192]{1,0:T(8,128)(2,1)} %li_ref.1, bf16[8,8192]{1,0:T(8,128)(2,1)} %oc_ref.1, bf16[128,1792]{1,0:T(8,128)(2,1)} %gate_ref.1, bf16[128,1792]{1,0:T(8,128)(2,1)} %up_ref.1, bf16[1792,8192]{1,0:T(8,128)(2,1)} %w_ref.1, bf16[8192,64]{1,0:T(8,128)(2,1)} %copy.13.piu_ref, ...), custom_call_target="tpu_custom_call" | custom-call | flops 3758096384 | bytes 29360128 | tf_op jit(solution)/shard_map/pallas_call | solution.py:263
  51.4 1.4 %copy.19 = bf16[1,8192]{1,0:T(2,128)(2,1)} copy(bf16[1,8192]{1,0:T(2,128)(2,1)} %get-tuple-element.4) | data formatting | bytes 32768
  52.8 1.2 %copy.20 = f32[1,32]{1,0:T(1,128)} copy(f32[1,32]{1,0:T(1,128)} %get-tuple-element.5) | data formatting | bytes 256
Async XLA Ops:
  0.6 4.0 %copy-start = (bf16[8192,64]{0,1:T(8,128)(2,1)S(1)}, bf16[8192,64]{0,1:T(8,128)(2,1)}, u32[]{:S(2)}) copy-start(bf16[8192,64]{0,1:T(8,128)(2,1)} %param.16) | copy-start | bytes 3145732
  0.6 5.8 %copy-start.1 = (bf16[8192,64]{0,1:T(8,128)(2,1)S(1)}, bf16[8192,64]{0,1:T(8,128)(2,1)}, u32[]{:S(2)}) copy-start(bf16[8192,64]{0,1:T(8,128)(2,1)} %param.19) | copy-start | bytes 3145732

commit v2 on v1

--- a/solution.py
+++ b/solution.py
@@ -27,9 +27,10 @@
     width = w.shape[2]
     half = width // 2
     feat = w.shape[1]
-    tile = 256 if feat % 256 == 0 else feat
+    tile = 896 if feat % 896 == 0 else feat
     tiles = feat // tile
-    side = pou.shape[1]
+    side = pou.shape[0]
+    nt = (((1,), (1,)), ((), ()))
     me = lax.axis_index("tensor")
     core = lax.rem(me, 2)
     b = lax.rem(me // 2, b_n)
@@ -53,10 +54,10 @@
 
     barrier = pltpu.get_barrier_semaphore()
 
-    @pl.loop(1, n)
-    def _(k):
-        pl.semaphore_signal(barrier, inc=1, device_id={"tensor": lax.rem(me + k, n)},
-                            device_id_type=pl.DeviceIdType.MESH)
+    near = [device(lax.rem(a + k, a_n), b, core) for k in range(1, a_n)]
+    near += [device(a, lax.rem(b + k, b_n), core) for k in range(1, b_n)] + [device(a, b, 1 - core)]
+    for peer in near:
+        pl.semaphore_signal(barrier, inc=1, device_id=peer, device_id_type=pl.DeviceIdType.MESH)
 
     local[0].wait()
     for c in range(chunks):
@@ -71,19 +72,20 @@
         qtmp[s * qn:(s + 1) * qn, :] = q[:, s * qw:(s + 1) * qw].astype(F32)
     g[chunks, slot] = qtmp[...].astype(BF16)
 
-    pl.semaphore_wait(barrier, n - 1)
-
-    def z_copy(c, k):
-        return pltpu.make_async_remote_copy(
-            src_ref=g.at[c, slot], dst_ref=g.at[c, slot],
-            send_sem=z_send.at[c, k], recv_sem=z_recv.at[c, k],
-            device_id=device(lax.rem(a + k, a_n), b, core), device_id_type=pl.DeviceIdType.MESH)
-
-    def x_copy(c, k):
-        column = pl.ds((core * b_n + b) * a_n, a_n)
-        return pltpu.make_async_remote_copy(
-            src_ref=g.at[c, column], dst_ref=g.at[c, column],
-            send_sem=x_send.at[c, k], recv_sem=x_recv.at[c, k],
+    pl.semaphore_wait(barrier, len(near))
+
+    base = (core * b_n + b) * a_n
+
+    def z_copy(c, s, to, relay=False):
+        return pltpu.make_async_remote_copy(
+            src_ref=g.at[c, base + s], dst_ref=g.at[c, base + s],
+            send_sem=z_send.at[c, a_n if relay else to], recv_sem=z_recv.at[c, s],
+            device_id=device(to, b, core), device_id_type=pl.DeviceIdType.MESH)
+
+    def x_copy(c, k, s):
+        return pltpu.make_async_remote_copy(
+            src_ref=g.at[c, base + s], dst_ref=g.at[c, base + s],
+            send_sem=x_send.at[c, k, s], recv_sem=x_recv.at[c, k, s],
             device_id=device(a, lax.rem(b + k, b_n), core), device_id_type=pl.DeviceIdType.MESH)
 
     def c_copy(c, k):
@@ -93,20 +95,46 @@
             send_sem=c_send.at[c, k], recv_sem=c_recv.at[c, k],
             device_id=device(a, b, 1 - core), device_id_type=pl.DeviceIdType.MESH)
 
+    steps = (1, -1, 2, -2)
+
+    def reach(step):
+        return (a + step >= 0) & (a + step < a_n)
+
+    def start(c):
+        for step in steps:
+            @pl.when(reach(step))
+            def _():
+                z_copy(c, a, a + step).start()
+        for k in range(1, b_n):
+            x_copy(c, k, a).start()
+
+    def relays(c, op):
+        for s, via, to in ((0, 2, 3), (3, 1, 0)):
+            @pl.when(a == via)
+            def _():
+                op(z_copy(c, s, to, True))
+
     for c in range(chunks + 1):
-        for k in range(1, a_n):
-            z_copy(c, k).start()
+        start(c)
 
     def forward_z(c):
-        for k in range(1, a_n):
-            z_copy(c, k).wait_recv()
-        for k in range(1, b_n):
-            x_copy(c, k).start()
+        for step in (1, -1, 2, -2, 3, -3):
+            @pl.when(reach(step))
+            def _():
+                s = a + step
+                z_copy(c, s, a).wait_recv()
+                for k in range(1, b_n):
+                    x_copy(c, k, s).start()
+            if step in (2, -2):
+                @pl.when(a == (1 if step == 2 else 2))
+                def _():
+                    z_copy(c, a + step, 0 if step == 2 else 3, True).start()
         c_copy(c, 0).start()
 
     def forward_x(c):
         for k in range(1, b_n):
-            x_copy(c, k).wait_recv()
+            for s in range(a_n):
+                x_copy(c, k, s).wait_recv()
             c_copy(c, k).start()
 
     def arrived(c):
@@ -121,15 +149,15 @@
         ga = v / (1.0 + jnp.exp(-v))
         act[:, sl] = ga
         hidden = (ga * up[:, sl].astype(F32)).astype(BF16)
-        d = jnp.dot(hidden, pid[sl, :], preferred_element_type=F32)
+        d = lax.dot_general(hidden, pid[:, sl], nt, preferred_element_type=F32)
         if i == 0:
             in_down[...] = d
         else:
             in_down[...] += d
     for i in (5, 6, 7):
         local[i].wait()
-    own_iu = jnp.dot(li[...], piu[...], preferred_element_type=F32)
-    own_od = jnp.dot(oc[...], pod[...], preferred_element_type=F32)
+    own_iu = lax.dot_general(li[...], piu[...], nt, preferred_element_type=F32)
+    own_od = lax.dot_general(oc[...], pod[...], nt, preferred_element_type=F32)
     own_u = jnp.concatenate([own_iu, own_od], axis=1)
     mine[...] = own_u
     all_u[me] = own_u
@@ -139,9 +167,10 @@
             src_ref=mine, dst_ref=all_u.at[me], send_sem=u_send.at[0], recv_sem=u_recv.at[0],
             device_id={"tensor": lax.rem(me + k, n)}, device_id_type=pl.DeviceIdType.MESH)
 
-    @pl.loop(1, n)
-    def _(k):
-        u_copy(k).start()
+    def send_u():
+        @pl.loop(1, n)
+        def _(k):
+            u_copy(k).start()
 
     def pack(c):
         @pl.loop(0, n // 2)
@@ -153,8 +182,6 @@
             x[at, 0:half] = jnp.concatenate([g0[0:8], g1[0:8]], axis=0).astype(BF16)
             x[at, half:width] = jnp.concatenate([g0[8:16], g1[8:16]], axis=0).astype(BF16)
 
-    nt = (((1,), (1,)), ((), ()))
-
     def multiply(c):
         w_copies[c].wait()
         arrived(c)
@@ -173,14 +200,18 @@
     for c in range(chunks):
         forward_z(c + 1)
         forward_x(c)
-        multiply(c)
+        if c > 0:
+            multiply(c - 1)
+        if c == 1:
+            send_u()
+    multiply(chunks - 1)
 
     local[8].wait()
     out_up = jnp.zeros((x.shape[0], side), F32)
     for i in range(tiles):
         sl = slice(i * tile, (i + 1) * tile)
         gu = (acc[i] * act[:, sl]).astype(BF16)
-        out_up += jnp.dot(gu, pou[sl, :], preferred_element_type=F32)
+        out_up += lax.dot_general(gu, pou[:, sl], nt, preferred_element_type=F32)
     part[...] = jnp.concatenate([out_up, in_down[...]], axis=1).reshape(part.shape)
 
     def r_copy(k):
@@ -239,10 +270,14 @@
     scores_ref[...] = jnp.sum(sc, axis=0, keepdims=True)
 
     for c in range(chunks + 1):
-        for k in range(1, a_n):
-            z_copy(c, k).wait_send()
+        for step in steps:
+            @pl.when(reach(step))
+            def _():
+                z_copy(c, a, a + step).wait_send()
+        relays(c, lambda copy: copy.wait_send())
         for k in range(1, b_n):
-            x_copy(c, k).wait_send()
+            for s in range(a_n):
+                x_copy(c, k, s).wait_send()
         for k in range(b_n):
             c_copy(c, k).wait_send()
     total(all_u, u_send, u_recv).wait_send()
@@ -253,8 +288,9 @@
     tokens, feat = gate.shape
     model = w.shape[1]
     side = piu.shape[1]
+    piu, pou, pid, pod = piu.T, pou.T, pid.T, pod.T
     width = model // CHUNKS
-    tile = 256 if feat % 256 == 0 else feat
+    tile = 896 if feat % 896 == 0 else feat
     b_n = n // (2 * OUTER)
     vm = pltpu.VMEM
     dma = pltpu.SemaphoreType.DMA
@@ -279,8 +315,8 @@
             vm((n, LEN, 2 * side), F32), vm((n, LEN, 2 * side), F32), vm((n, LEN, 2 * side), F32),
             vm((16, q.shape[1] * qn // 16), F32), vm((16 // qn, q.shape[1] * qn // 16), F32),
             dma((9,)), dma((CHUNKS,)),
-            dma((CHUNKS + 1, OUTER)), dma((CHUNKS + 1, OUTER)),
-            dma((CHUNKS + 1, b_n)), dma((CHUNKS + 1, b_n)),
+            dma((CHUNKS + 1, OUTER + 1)), dma((CHUNKS + 1, OUTER)),
+            dma((CHUNKS + 1, b_n, OUTER)), dma((CHUNKS + 1, b_n, OUTER)),
             dma((CHUNKS + 1, b_n)), dma((CHUNKS + 1, b_n)),
             dma((1,)), dma((1,)), dma((1,)), dma((1,)),
         ],

time: 54.3 us -> 42.3 us (0.78)
  local copies, waits for them, and re-layouts: 10.2 us -> 2.58 us
  Pallas kernels: 43.2 us -> 38.9 us
    unnamed x10 -> x2, local copies, waits for them, and re-layouts: 10.2 us -> 2.58 us
    pallas_call x1, Pallas kernels: 43.2 us -> 38.9 us  [shards(): pl.pallas_call(functools.partial(kernel, n), out_shape=(jax.ShapeDtypeStr...]
where the time goes in v2:
time: 42.3 us; the launch traced here: 42.1 us
  Pallas kernels  38.9 us (92%)
  local copies, waits for them, and re-layouts  2.58 us (6%)
  between operations  0.64 us (2%)
    pallas_call x1, Pallas kernels, shards(): pl.pallas_call(functools.partial(kernel, n), out_shape=(jax.ShapeDtypeStr...  38.9 us
    unnamed x2, local copies, waits for them, and re-layouts  2.58 us

profile of v2, /device:TPU:0, one launch (start us, length us, event | category | flops | bytes accessed | tf_op | source)
XLA Modules:
  0.0 42.1 jit_solution(986385249223991889)
XLA Ops:
  0.6 38.9 %shard_map.122 = (bf16[1,8192]{1,0:T(2,128)(2,1)}, f32[1,32]{1,0:T(1,128)}) custom-call(bf16[8,8192]{1,0:T(8,128)(2,1)} %li_ref.1, bf16[8,8192]{1,0:T(8,128)(2,1)} %oc_ref.1, bf16[128,1792]{1,0:T(8,128)(2,1)} %gate_ref.1, bf16[128,1792]{1,0:T(8,128)(2,1)} %up_ref.1, bf16[1792,8192]{1,0:T(8,128)(2,1)} %w_ref.1, bf16[64,8192]{1,0:T(8,128)(2,1)} %bitcast.4, ...), custom_call_target="tpu_custom_call" | custom-call | flops 3758096384 | bytes 29360128 | tf_op jit(solution)/shard_map/pallas_call | solution.py:299
  39.5 1.4 %copy.15 = bf16[1,8192]{1,0:T(2,128)(2,1)} copy(bf16[1,8192]{1,0:T(2,128)(2,1)} %get-tuple-element.4) | data formatting | bytes 32768
  40.9 1.2 %copy.16 = f32[1,32]{1,0:T(1,128)} copy(f32[1,32]{1,0:T(1,128)} %get-tuple-element.5) | data formatting | bytes 256
